TPU v7x, 32 devices: a whole 2x2x4 slice. The times are simulated.
32 devices in a mesh: dp: 16 (over z, y, core), mp: 2 (over x).
Axes of the slice: x: 2, y: 2, z: 4, core: 2. Of those that a mesh axis runs over, the one named last changes fastest.
Arguments:
- residual_in: bfloat16 [8192, 1024], P(('dp', 'mp')), may hold values from -6 to 6
- cotangent: bfloat16 [8192, 1024], P(('dp', 'mp')), may hold values from -6 to 6
- ln_gain: float32 [1024], replicated, may hold values from 0.5 to 1.5
- ln_bias: float32 [1024], replicated, may hold values from -3 to 3
- w_qkv: bfloat16 [3, 1024, 1024], P(None, 'dp', 'mp'), may hold values from -0.1875 to 0.1875
- w_out: bfloat16 [1024, 1024], P('mp', 'dp'), may hold values from -1.5 to 1.5
- w_in: bfloat16 [1024, 4096], P('dp', 'mp'), may hold values from -0.1875 to 0.1875
- b_in: bfloat16 [4096], P(('mp', 'dp')), may hold values from -3 to 3
- w_back: bfloat16 [4096, 1024], P('mp', 'dp'), may hold values from -0.09375 to 0.09375
- b_back: float32 [1024], replicated, may hold values from -3 to 3
- bucket_ids: int32 [16], P('dp'), may hold values from 0 to 3, as said below
- residue_counts: int32 [16, 16], P('dp'), may hold values from 30 to 256
Outputs:
- block_out: bfloat16 [8192, 1024], P(('dp', 'mp'))
- grad_input: bfloat16 [8192, 1024], P(('dp', 'mp'))
- grad_ln_gain: float32 [1024], P(('dp', 'mp'))
- grad_ln_bias: float32 [1024], P(('dp', 'mp'))
- grad_w_qkv: float32 [3, 1024, 1024], P(None, 'dp', 'mp')
- grad_w_out: float32 [1024, 1024], P('mp', 'dp')
- grad_w_in: float32 [1024, 4096], P('dp', 'mp')
- grad_b_in: float32 [4096], P(('mp', 'dp'))
- grad_w_back: float32 [4096, 1024], P('mp', 'dp')
- grad_b_back: float32 [1024], P(('dp', 'mp'))
Inputs may be any that keep to these rules, and one draw needn't show every extreme that they name: `bucket_ids`: every bucket number is held by the same number of groups.
All inputs are finite; a program needn't handle non-finite values.
Results may differ from a plain program's by a relative error of at most 0.017.
Values may be sent and summed in bfloat16 or wider, within the bound.
A program may use at most 192 MiB of HBM per device.

v0:
```python
from functools import partial

import jax
import jax.numpy as jnp
from jax import lax
from jax.sharding import PartitionSpec as P

HD = 64
ROT = 32
SLOTS = 16


NORM_EPS = 1e-05
MASKED_SCORE = -1e30


def norm_rows(inputs_now, norm_gain, norm_shift):
    centred = inputs_now - jnp.mean(inputs_now, axis=-1, keepdims=True)
    spread = jnp.mean(centred * centred, axis=-1, keepdims=True)
    return centred * lax.rsqrt(spread + NORM_EPS) * norm_gain + norm_shift


def slot_tables(bucket_one, residue_row, group_rows):
    slot_length = jnp.right_shift(jnp.int32(group_rows // 2), bucket_one)
    places = jnp.arange(group_rows, dtype=jnp.int32)
    slot_ids = places // slot_length
    inside = places - slot_ids * slot_length
    match_table = slot_ids[:, None] == jnp.arange(SLOTS, dtype=jnp.int32)[None, :]
    picked = jnp.sum(jnp.where(match_table, residue_row[None, :], 0), axis=1)
    live_rows = jnp.minimum(picked, slot_length)
    return (slot_ids, inside, inside < live_rows)


def rope_tables(inside):
    half_steps = jnp.arange(ROT // 2, dtype=jnp.float32)
    inverse_rates = 10000.0 ** (-2.0 * half_steps / ROT)
    angles = inside.astype(jnp.float32)[:, None] * inverse_rates[None, :]
    return (jnp.cos(angles), jnp.sin(angles))


def rotate(values, cosine_table, sine_table):
    row_count = values.shape[0]
    head_count = values.shape[1]
    paired = values[..., :ROT].reshape(row_count, head_count, ROT // 2, 2)
    even_part = paired[..., 0]
    odd_part = paired[..., 1]
    cosine_now = cosine_table[:, None, :]
    sine_now = sine_table[:, None, :]
    turned = jnp.stack(
        [
            even_part * cosine_now - odd_part * sine_now,
            odd_part * cosine_now + even_part * sine_now,
        ],
        axis=-1,
    )
    return jnp.concatenate([turned.reshape(row_count, head_count, ROT), values[..., ROT:]], axis=-1)


def mask_block(block_start, block_rows, slot_ids):
    query_places = block_start + jnp.arange(block_rows, dtype=jnp.int32)
    query_slots = lax.dynamic_slice_in_dim(slot_ids, block_start, block_rows, 0)
    key_places = jnp.arange(slot_ids.shape[0], dtype=jnp.int32)
    return (query_slots[:, None] == slot_ids[None, :]) & (
        key_places[None, :] <= query_places[:, None]
    )


def over_rows(first_op, second_op):
    return lax.dot_general(
        first_op, second_op, (((0,), (0,)), ((), ())), preferred_element_type=jnp.float32
    )


def against_weight(first_op, second_op):
    return lax.dot_general(
        first_op, second_op, (((1,), (1,)), ((), ())), preferred_element_type=jnp.float32
    )


def on_device(
    residual_in,
    cotangent,
    ln_gain,
    ln_bias,
    w_qkv,
    w_out,
    w_in,
    b_in,
    w_back,
    b_back,
    bucket_ids,
    residue_counts,
):
    model_count = lax.axis_size("mp")
    model_rank = lax.axis_index("mp")
    local_rows = residual_in.shape[0]
    group_rows = local_rows * model_count
    slot_ids, inside, valid_rows = slot_tables(bucket_ids[0], residue_counts[0], group_rows)
    cosine_table, sine_table = rope_tables(inside)
    qkv_all, out_all, in_all, bias_in, back_all = (
        lax.all_gather(w_qkv, "dp", axis=1, tiled=True),
        lax.all_gather(w_out, "dp", axis=1, tiled=True),
        lax.all_gather(w_in, "dp", axis=0, tiled=True),
        lax.all_gather(b_in, "dp", axis=0, tiled=True),
        lax.all_gather(w_back, "dp", axis=1, tiled=True),
    )
    x_local = residual_in.astype(jnp.float32)
    x_group = lax.all_gather(residual_in, "mp", axis=0, tiled=True).astype(jnp.float32)
    normed = norm_rows(x_group, ln_gain, ln_bias).astype(jnp.bfloat16)
    head_width = qkv_all.shape[2]
    head_count = head_width // HD
    score_scale = HD ** (-0.5)

    def project(member_index):
        return jnp.dot(normed, qkv_all[member_index], preferred_element_type=jnp.float32).reshape(
            group_rows, head_count, HD
        )

    queries = rotate(project(0), cosine_table, sine_table).astype(jnp.bfloat16)
    key_rows = rotate(project(1), cosine_table, sine_table).astype(jnp.bfloat16)
    value_rows = project(2).astype(jnp.bfloat16)
    block_rows = min(512, group_rows)
    starts = jnp.arange(group_rows // block_rows, dtype=jnp.int32) * block_rows

    def block_scores(block_start):
        query_block = lax.dynamic_slice_in_dim(queries, block_start, block_rows, 0)
        allowed = mask_block(block_start, block_rows, slot_ids)
        scores = (
            jnp.einsum("qhd,khd->hqk", query_block, key_rows, preferred_element_type=jnp.float32)
            * score_scale
        )
        return (query_block, jnp.where(allowed[None], scores, MASKED_SCORE))

    def forward_block(block_start):
        query_block, scores = block_scores(block_start)
        row_peak = jnp.max(scores, axis=-1, keepdims=True)
        exp_scores = jnp.exp(scores - row_peak)
        row_total = jnp.sum(exp_scores, axis=-1, keepdims=True)
        weights_now = (exp_scores / row_total).astype(jnp.bfloat16)
        attended = jnp.einsum(
            "hqk,khd->qhd", weights_now, value_rows, preferred_element_type=jnp.float32
        )
        return (attended.astype(jnp.bfloat16), (row_peak + jnp.log(row_total))[..., 0])

    attended_blocks, log_totals = lax.map(forward_block, starts)
    mixed_rows = attended_blocks.reshape(group_rows, head_width)
    hidden = jnp.dot(normed, in_all, preferred_element_type=jnp.float32) + bias_in.astype(
        jnp.float32
    )
    gelu_tanh = partial(jax.nn.gelu, approximate=True)
    active_value, gelu_pull = jax.vjp(gelu_tanh, hidden)
    active = active_value.astype(jnp.bfloat16)
    partial_out = jnp.dot(mixed_rows, out_all, preferred_element_type=jnp.float32) + jnp.dot(
        active, back_all, preferred_element_type=jnp.float32
    )
    summed_all = lax.psum(partial_out.astype(jnp.bfloat16), "mp").astype(jnp.float32)
    summed = lax.dynamic_slice_in_dim(summed_all, model_rank * local_rows, local_rows, 0)
    block_out = (x_local + summed + b_back).astype(jnp.bfloat16)
    cot_group = lax.all_gather(cotangent, "mp", axis=0, tiled=True)
    seed_rows = jnp.where(valid_rows[:, None], cot_group, jnp.zeros_like(cot_group))
    qkv_all, out_all, in_all, back_all = (
        lax.all_gather(w_qkv, "dp", axis=1, tiled=True),
        lax.all_gather(w_out, "dp", axis=1, tiled=True),
        lax.all_gather(w_in, "dp", axis=0, tiled=True),
        lax.all_gather(w_back, "dp", axis=1, tiled=True),
    )
    active_grad = against_weight(seed_rows, back_all)
    hidden_grad = gelu_pull(active_grad)[0].astype(jnp.bfloat16)
    grad_in_local = over_rows(normed, hidden_grad)
    grad_bias_in = jnp.sum(hidden_grad.astype(jnp.float32), axis=0)
    grad_back_local = over_rows(active, seed_rows)
    grad_out_local = over_rows(mixed_rows, seed_rows)
    normed_grad = against_weight(hidden_grad, in_all)
    mixed_grad = (
        against_weight(seed_rows, out_all).astype(jnp.bfloat16).reshape(group_rows, head_count, HD)
    )

    def backward_block(carry, inputs_now):
        key_acc, value_acc = carry
        block_start, log_total = inputs_now
        query_block, scores = block_scores(block_start)
        grad_block = lax.dynamic_slice_in_dim(mixed_grad, block_start, block_rows, 0)
        probs = jnp.exp(scores - log_total[..., None])
        probs_low = probs.astype(jnp.bfloat16)
        value_acc = value_acc + jnp.einsum(
            "hqk,qhd->khd", probs_low, grad_block, preferred_element_type=jnp.float32
        )
        probs_grad = jnp.einsum(
            "qhd,khd->hqk", grad_block, value_rows, preferred_element_type=jnp.float32
        )
        score_grad = probs * (probs_grad - jnp.sum(probs * probs_grad, axis=-1, keepdims=True))
        score_low = score_grad.astype(jnp.bfloat16)
        query_grad = (
            jnp.einsum("hqk,khd->qhd", score_low, key_rows, preferred_element_type=jnp.float32)
            * score_scale
        )
        key_acc = (
            key_acc
            + jnp.einsum("hqk,qhd->khd", score_low, query_block, preferred_element_type=jnp.float32)
            * score_scale
        )
        return ((key_acc, value_acc), query_grad)

    empty_heads = jnp.zeros((group_rows, head_count, HD), jnp.float32)
    (key_acc, value_acc), query_blocks = lax.scan(
        backward_block, (empty_heads, empty_heads), (starts, log_totals)
    )
    turn_back = partial(rotate, cosine_table=cosine_table, sine_table=sine_table)
    unturn = jax.vjp(turn_back, empty_heads)[1]
    query_pre_grad = (
        unturn(query_blocks.reshape(group_rows, head_count, HD))[0]
        .astype(jnp.bfloat16)
        .reshape(group_rows, head_width)
    )
    key_pre_grad = unturn(key_acc)[0].astype(jnp.bfloat16).reshape(group_rows, head_width)
    value_grad = value_acc.astype(jnp.bfloat16).reshape(group_rows, head_width)
    grad_qkv_local = jnp.stack(
        [
            over_rows(normed, query_pre_grad),
            over_rows(normed, key_pre_grad),
            over_rows(normed, value_grad),
        ],
        axis=0,
    )
    normed_grad = (
        normed_grad
        + against_weight(query_pre_grad, qkv_all[0])
        + against_weight(key_pre_grad, qkv_all[1])
        + against_weight(value_grad, qkv_all[2])
    )
    share_grad = lax.psum(normed_grad.astype(jnp.bfloat16), "mp").astype(jnp.float32)
    seed_group = seed_rows.astype(jnp.float32)
    norm_pull = jax.vjp(norm_rows, x_group, ln_gain, ln_bias)[1]
    input_part, gain_part, shift_part = norm_pull(share_grad)
    input_group = seed_group + input_part
    grad_input = lax.dynamic_slice_in_dim(
        input_group, model_rank * local_rows, local_rows, 0
    ).astype(jnp.bfloat16)
    back_part = jnp.sum(seed_group, axis=0)
    grad_w_qkv, grad_w_out, grad_w_in, grad_b_in, grad_w_back, gain_rows, shift_rows, back_rows = (
        lax.psum_scatter(
            grad_qkv_local.astype(jnp.bfloat16), "dp", scatter_dimension=1, tiled=True
        ).astype(jnp.float32),
        lax.psum_scatter(
            grad_out_local.astype(jnp.bfloat16), "dp", scatter_dimension=1, tiled=True
        ).astype(jnp.float32),
        lax.psum_scatter(
            grad_in_local.astype(jnp.bfloat16), "dp", scatter_dimension=0, tiled=True
        ).astype(jnp.float32),
        lax.psum_scatter(
            grad_bias_in.astype(jnp.bfloat16), "dp", scatter_dimension=0, tiled=True
        ).astype(jnp.float32),
        lax.psum_scatter(
            grad_back_local.astype(jnp.bfloat16), "dp", scatter_dimension=1, tiled=True
        ).astype(jnp.float32),
        lax.psum_scatter(
            gain_part.astype(jnp.bfloat16), "dp", scatter_dimension=0, tiled=True
        ).astype(jnp.float32),
        lax.psum_scatter(
            shift_part.astype(jnp.bfloat16), "dp", scatter_dimension=0, tiled=True
        ).astype(jnp.float32),
        lax.psum_scatter(
            back_part.astype(jnp.bfloat16), "dp", scatter_dimension=0, tiled=True
        ).astype(jnp.float32),
    )
    piece_width = gain_rows.shape[0] // model_count
    grad_ln_gain = lax.dynamic_slice_in_dim(gain_rows, model_rank * piece_width, piece_width, 0)
    grad_ln_bias = lax.dynamic_slice_in_dim(shift_rows, model_rank * piece_width, piece_width, 0)
    grad_b_back = lax.dynamic_slice_in_dim(back_rows, model_rank * piece_width, piece_width, 0)
    return (
        block_out,
        grad_input,
        grad_ln_gain,
        grad_ln_bias,
        grad_w_qkv,
        grad_w_out,
        grad_w_in,
        grad_b_in,
        grad_w_back,
        grad_b_back,
    )


def solution(mesh):
    placed = (
        P(("dp", "mp"), None),
        P(("dp", "mp"), None),
        P(),
        P(),
        P(None, "dp", "mp"),
        P("mp", "dp"),
        P("dp", "mp"),
        P(("mp", "dp")),
        P("mp", "dp"),
        P(),
        P("dp"),
        P("dp", None),
    )
    return jax.shard_map(
        on_device,
        mesh=mesh,
        in_specs=placed,
        out_specs=(
            P(("dp", "mp"), None),
            P(("dp", "mp"), None),
            P(("dp", "mp")),
            P(("dp", "mp")),
            P(None, "dp", "mp"),
            P("mp", "dp"),
            P("dp", "mp"),
            P(("mp", "dp")),
            P("mp", "dp"),
            P(("dp", "mp")),
        ),
        check_vma=False,
    )
```

profile of v0, /device:TPU:0, one launch (start us, length us, event | category | flops | bytes accessed | tf_op | source)
XLA Modules:
  0.0 599.4 jit_solution(7787705663513097953)
XLA Ops:
  13.9 23.2 %all-gather = bf16[16,1,128]{2,1,0:T(2,128)(2,1)S(1)} all-gather(bf16[1,1,128]{2,1,0:T(2,128)(2,1)} %bitcast.114), channel_id=1, replica_groups=mesh['dp'=16,'mp'=2] {'dp'}, dimensions={0}, use_global_device_ids=true | all-gather | bytes 4352 | tf_op jit(solution)/shard_map/all_gather | solution.py:104
  37.3 1.4 convert_reduce_fusion
  38.7 1.6 fusion.21
  40.4 16.1 %all-gather.18.cloned.1.call-done = bf16[512,1024]{1,0:T(8,128)(2,1)} async-done(((bf16[256,1024]{1,0:T(8,128)(2,1)}), bf16[512,1024]{1,0:T(8,128)(2,1)}) %all-gather.18.cloned.1.call-update) | async-done | bytes 1048592 | tf_op jit(solution)/shard_map/all_gather | solution.py:159
  56.5 1.5 fusion.65
  58.0 38.6 %all-gather.12.cloned.1.call-done = bf16[512,1024]{0,1:T(8,128)(2,1)} async-done(((bf16[512,64]{0,1:T(8,128)(2,1)}), bf16[512,1024]{0,1:T(8,128)(2,1)}) %all-gather.12.cloned.1.call-update) | async-done | bytes 1048592 | tf_op jit(solution)/shard_map/all_gather | solution.py:102
  96.6 2.8 convolution_convert_fusion.6
  99.4 43.4 %all-gather.10.cloned.1.call-done = bf16[3,1024,512]{2,1,0:T(8,128)(2,1)} async-done(((bf16[3,64,512]{2,1,0:T(8,128)(2,1)}), bf16[3,1024,512]{2,1,0:T(8,128)(2,1)}) %all-gather.10.cloned.1.call-update) | async-done | bytes 3145744 | tf_op jit(solution)/shard_map/all_gather | solution.py:101
  142.8 3.1 slice_bitcast_fusion.1
  145.9 2.4 copy.37
  148.3 2.1 fusion.42
  153.4 2.2 fusion.40
  158.4 1.4 subtract_convert_fusion.1
  161.2 2.6 fusion.71
  166.8 2.2 multiply_reduce_fusion
  169.0 2.8 multiply_convert_fusion
  171.8 1.4 fusion.24
  174.1 3.1 fusion.25
  178.2 1.3 reshape.266
  179.6 1.9 multiply_add_fusion.3
  182.3 2.2 pad_add_fusion
  184.5 1.5 reshape.270
  185.9 5.2 fusion.29
  192.0 1.8 convolution_convert_fusion.2
  193.7 5.6 fusion.30
  202.7 2.1 fusion.35
  204.8 6.6 %fusion.60 = f32[512,2048]{1,0:T(8,128)} fusion(bf16[1024,2048]{1,0:T(8,128)(2,1)} %all-gather.14.cloned.1.call-done, bf16[512,1024]{1,0:T(8,128)(2,1)S(1)} %copy-done.2, f32[1024]{0:T(1024)S(1)} %copy-done.30, f32[1024]{0:T(1024)S(1)} %copy-done.26, f32[512]{0:T(512)S(1)} %fusion.50, f32[512]{0:T(512)S(1)} %broadcast_multiply_fusion), kind=kOutput, calls=%fused_computation.124 | convolution fusion | flops 2150629376 | bytes 9449472 | tf_op jit(solution)/shard_map/dot_general | solution.py:147
  211.4 34.2 %all-gather.16.cloned.1.call-done = bf16[2048,1024]{0,1:T(8,128)(2,1)} async-done(((bf16[2048,64]{0,1:T(8,128)(2,1)}), bf16[2048,1024]{0,1:T(8,128)(2,1)}) %all-gather.16.cloned.1.call-update) | async-done | bytes 4194320 | tf_op jit(solution)/shard_map/all_gather | solution.py:105
  245.7 8.6 %fusion.66 = (bf16[2048]{0:T(1024)(128)(2,1)S(1)}, bf16[512,2048]{1,0:T(8,128)(2,1)S(1)}) fusion(f32[512,2048]{1,0:T(8,128)} %fusion.60, f32[2048]{0:T(1024)S(1)} %bitcast.110, bf16[512,1024]{1,0:T(8,128)(2,1)} %copy-done.6, bf16[2048,1024]{0,1:T(8,128)(2,1)} %all-gather.16.cloned.1.call-done), kind=kOutput, calls=%fused_computation.126 | convolution fusion | flops 2170550272 | bytes 11546624 | tf_op jit(solution)/shard_map/dot_general | solution.py:75
  254.3 2.8 fusion.55
  257.2 1.8 add_convert_fusion.1
  259.8 2.6 fusion.72
  262.4 3.0 add_convert_fusion
  265.5 2.1 fusion.28
  269.7 2.0 pad_maximum_fusion
  272.9 6.8 %convolution_convert_fusion = bf16[2048,1024]{0,1:T(8,128)(2,1)} fusion(bf16[512,1024]{1,0:T(8,128)(2,1)S(1)} %copy-done.8, f32[512,2048]{1,0:T(8,128)} %fusion.60, f32[2048]{0:T(1024)S(1)} %bitcast.112), kind=kOutput, calls=%fused_computation.21 | convolution fusion | flops 2160066560 | bytes 9445376 | tf_op jit(solution)/shard_map/dot_general | solution.py:69
  279.7 6.1 %convolution_convert_fusion.1 = bf16[1024,2048]{1,0:T(8,128)(2,1)} fusion(bf16[512,2048]{1,0:T(8,128)(2,1)} %copy-done.32, bf16[512,1024]{1,0:T(8,128)(2,1)S(1)} %copy-done.2, f32[1024]{0:T(1024)S(1)} %copy-done.30, f32[1024]{0:T(1024)S(1)} %copy-done.26, f32[512]{0:T(512)S(1)} %fusion.50, f32[512]{0:T(512)S(1)} %broadcast_multiply_fusion), kind=kOutput, calls=%fused_computation.22 | convolution fusion | flops 2152726528 | bytes 7352320 | tf_op jit(solution)/shard_map/dot_general | solution.py:69
  288.4 16.8 %reduce-scatter.7.cloned.1.call-done = bf16[512,64]{0,1:T(8,128)(2,1)} async-done(((bf16[512,1024]{0,1:T(8,128)(2,1)}), bf16[512,64]{0,1:T(8,128)(2,1)}) %reduce-scatter.7.cloned.1.call-update) | async-done | bytes 65552 | tf_op jit(solution)/shard_map/reduce_scatter | solution.py:244
  305.2 1.5 convert_element_type.156
  306.7 63.1 %all-reduce.16.cloned.1.call-done = (bf16[512,1024]{1,0:T(8,128)(2,1)}, bf16[512,1024]{1,0:T(8,128)(2,1)}) async-done(((bf16[512,1024]{1,0:T(8,128)(2,1)}, bf16[512,1024]{1,0:T(8,128)(2,1)}), (bf16[512,1024]{1,0:T(8,128)(2,1)}, bf16[512,1024]{1,0:T(8,128)(2,1)})) %all-reduce.16.cloned.1.call-update) | async-done | bytes 2097168 | tf_op jit(solution)/shard_map/psum | solution.py:156
  369.8 1.5 reduce_sum.142
  371.3 2.2 fusion.23
  373.5 61.8 %all-reduce.12 = (bf16[1024]{0:T(1024)(128)(2,1)S(1)}, bf16[1024]{0:T(1024)(128)(2,1)S(1)}, bf16[2048]{0:T(1024)(128)(2,1)S(1)}, bf16[1024]{0:T(1024)(128)(2,1)S(1)}) all-reduce(bf16[1024]{0:T(1024)(128)(2,1)S(1)} %get-tuple-element.51, bf16[1024]{0:T(1024)(128)(2,1)S(1)} %reduce_sum.142, ...), channel_id=2, replica_groups=mesh['dp'=16,'mp'=2] {'dp'}, use_global_device_ids=true, to_apply=%region_11.12.clone | all-reduce | flops 5120 | bytes 20480
  440.8 1.7 convert_element_type.154
  442.5 72.6 %reduce-scatter.11.cloned.1.call-done = bf16[2048,64]{0,1:T(8,128)(2,1)} async-done(((bf16[2048,1024]{0,1:T(8,128)(2,1)}), bf16[2048,64]{0,1:T(8,128)(2,1)}) %reduce-scatter.11.cloned.1.call-update) | async-done | bytes 262160 | tf_op jit(solution)/shard_map/reduce_scatter | solution.py:253
  515.1 1.8 convert_element_type.161
  516.9 74.1 %reduce-scatter.9.cloned.1.call-done = bf16[64,2048]{1,0:T(8,128)(2,1)} async-done(((bf16[1024,2048]{1,0:T(8,128)(2,1)}), bf16[64,2048]{1,0:T(8,128)(2,1)}) %reduce-scatter.9.cloned.1.call-update) | async-done | bytes 262160 | tf_op jit(solution)/shard_map/reduce_scatter | solution.py:247
  590.9 1.8 convert_element_type.158
  (141 shorter events, 34.0 us)
Async XLA Ops:
  7.2 30.1 %all-gather.8.cloned.1.call-start = ((), (), s32[]{:S(2)}) async-start(), calls=%async_computation.4 | async-start | bytes 1572864 | tf_op jit(solution)/shard_map/all_gather | solution.py:108
  7.9 48.6 %all-gather.18.cloned.1.call-start = ((), (), s32[]{:S(2)}) async-start(), calls=%async_computation.9 | async-start | bytes 1572864 | tf_op jit(solution)/shard_map/all_gather | solution.py:159
  8.7 88.0 %all-gather.12.cloned.1.call-start = ((), (), s32[]{:S(2)}) async-start(), calls=%async_computation.6 | async-start | bytes 1114112 | tf_op jit(solution)/shard_map/all_gather | solution.py:102
  9.4 133.4 %all-gather.10.cloned.1.call-start = ((), (), s32[]{:S(2)}) async-start(), calls=%async_computation.5 | async-start | bytes 3342336 | tf_op jit(solution)/shard_map/all_gather | solution.py:101
  10.0 194.8 %all-gather.14.cloned.1.call-start = ((), (), s32[]{:S(2)}) async-start(), calls=%async_computation.7 | async-start | bytes 4456448 | tf_op jit(solution)/shard_map/all_gather | solution.py:103
  10.6 235.1 %all-gather.16.cloned.1.call-start = ((), (), s32[]{:S(2)}) async-start(), calls=%async_computation.8 | async-start | bytes 4456448 | tf_op jit(solution)/shard_map/all_gather | solution.py:105
  11.1 294.1 %reduce-scatter.7.cloned.1.call-start = ((), (), s32[]{:S(2)}) async-start(), calls=%async_computation.11 | async-start | bytes 1114112 | tf_op jit(solution)/shard_map/reduce_scatter | solution.py:244
  58.0 38.6 %copy-start.6 = (bf16[512,1024]{1,0:T(8,128)(2,1)}, bf16[512,1024]{1,0:T(8,128)(2,1)S(1)}, u32[]{:S(2)}) copy-start(bf16[512,1024]{1,0:T(8,128)(2,1)S(1)} %get-tuple-element.70) | copy-start | bytes 3145732
  99.4 48.9 %copy-start.2 = (bf16[512,1024]{1,0:T(8,128)(2,1)S(1)}, bf16[512,1024]{1,0:T(8,128)(2,1)}, u32[]{:S(2)}) copy-start(bf16[512,1024]{1,0:T(8,128)(2,1)} %all-gather.8.cloned.1.call-done) | copy-start | bytes 3145732
  99.4 48.9 %copy-start.26 = (f32[1024]{0:T(1024)S(1)}, f32[1024]{0:T(1024)}, u32[]{:S(2)}) copy-start(f32[1024]{0:T(1024)} %param.14) | copy-start | bytes 12292
  99.4 48.9 %copy-start.30 = (f32[1024]{0:T(1024)S(1)}, f32[1024]{0:T(1024)}, u32[]{:S(2)}) copy-start(f32[1024]{0:T(1024)} %param.15) | copy-start | bytes 12292
  153.4 2.3 copy-start.16
  156.8 1.6 copy-start.17
  158.1 3.1 copy-start.18
  161.2 2.6 copy-start.19
  163.8 5.2 copy-start
  163.8 2.0 copy-start.20
  165.0 1.7 copy-start.9
  166.7 2.2 copy-start.22
  171.8 2.0 copy-start.1
  185.9 6.0 %copy-start.7 = (bf16[512,1024]{1,0:T(8,128)(2,1)S(1)}, bf16[512,1024]{1,0:T(8,128)(2,1)}, u32[]{:S(2)}) copy-start(bf16[512,1024]{1,0:T(8,128)(2,1)} %copy-done.6) | copy-start | bytes 3145732
  191.2 0.8 copy-start.23
  199.3 170.5 %all-reduce.16.cloned.1.call-start = ((), (), s32[]{:S(2)}) async-start(), calls=%async_computation.14 | async-start | bytes 4194304 | tf_op jit(solution)/shard_map/psum | solution.py:156
  199.8 2.1 copy-start.3
  201.1 0.8 copy-start.11
  201.2 1.5 copy-start.13
  245.7 8.6 %copy-start.29 = (bf16[2048,1024]{0,1:T(8,128)(2,1)S(1)}, bf16[2048,1024]{0,1:T(8,128)(2,1)}, u32[]{:S(2)}) copy-start(bf16[2048,1024]{0,1:T(8,128)(2,1)} %all-gather.16.cloned.1.call-done) | copy-start | bytes 12582916
  245.7 8.6 %copy-start.33 = (f32[512,2048]{1,0:T(8,128)S(1)}, f32[512,2048]{1,0:T(8,128)}, u32[]{:S(2)}) copy-start(f32[512,2048]{1,0:T(8,128)} %fusion.60) | copy-start | bytes 12582916
  254.3 4.7 copy-start.32
  254.3 2.8 copy-start.21
  254.3 2.8 copy-start.24
  257.2 2.6 copy-start.28
  259.8 2.6 copy-start.5
  259.8 2.6 copy-start.10
  265.4 2.2 copy-start.14
  265.5 175.3 %reduce-scatter.5.cloned.1.call-start = ((), (), s32[]{:S(2)}) async-start(), calls=%async_computation.10 | async-start | bytes 3342336 | tf_op jit(solution)/shard_map/reduce_scatter | solution.py:241
  267.6 1.0 copy-start.12
  271.7 1.2 copy-start.8
  271.7 243.4 %reduce-scatter.11.cloned.1.call-start = ((), (), s32[]{:S(2)}) async-start(), calls=%async_computation.13 | async-start | bytes 4456448 | tf_op jit(solution)/shard_map/reduce_scatter | solution.py:253
  279.7 311.2 %reduce-scatter.9.cloned.1.call-start = ((), (), s32[]{:S(2)}) async-start(), calls=%async_computation.12 | async-start | bytes 4456448 | tf_op jit(solution)/shard_map/reduce_scatter | solution.py:247
  285.9 0.7 copy-start.31
  369.8 67.4 %copy-start.4 = (bf16[512,1024]{1,0:T(8,128)(2,1)S(1)}, bf16[512,1024]{1,0:T(8,128)(2,1)}, u32[]{:S(2)}) copy-start(bf16[512,1024]{1,0:T(8,128)(2,1)} %get-tuple-element.68) | copy-start | bytes 3145732
  437.3 2.5 copy-start.15
  437.3 2.5 copy-start.25
  437.3 2.5 copy-start.27
Sparse Core Ops, SparseCore 0:
  9.6 23.9 all-gather.7
  35.1 21.2 all-gather.17
  58.6 37.9 all-gather.11
  98.7 44.1 all-gather.9
  144.8 49.5 all-gather.13
  196.4 49.1 all-gather.15
  249.3 55.9 reduce-scatter.6
  307.7 62.0 all-reduce.15
  373.6 66.3 reduce-scatter.4
  443.8 71.2 reduce-scatter.10
  519.5 71.4 reduce-scatter.8
where the time goes:
time: 603 us; the launch traced here: 599 us
  waiting for transfers between devices  363 us (60%)
  blocking collectives  84.9 us (14%)
  matrix products  75 us (12%)
  other arithmetic  35.3 us (6%)
  local copies, waits for them, and re-layouts  24 us (4%)
  between operations  16.6 us (3%)
    reduce_scatter x1, waiting for transfers between devices, on_device(): lax.psum_scatter(grad_in_local.astype(jnp.bfloat16), 'dp', scatter_dimens...  74.1 us
    reduce_scatter x1, waiting for transfers between devices, on_device(): lax.psum_scatter(grad_back_local.astype(jnp.bfloat16), 'dp', scatter_dime...  72.6 us
    psum x1, waiting for transfers between devices, on_device(): lax.psum(partial_out.astype(jnp.bfloat16), 'mp').astype(jnp.float32)  63.1 us
    unnamed x1, blocking collectives  61.8 us
    all_gather x1, waiting for transfers between devices, on_device(): lax.all_gather(w_qkv, 'dp', axis=1, tiled=True)  43.4 us
    all_gather x1, waiting for transfers between devices, on_device(): lax.all_gather(w_out, 'dp', axis=1, tiled=True)  38.6 us
    all_gather x1, waiting for transfers between devices, on_device(): lax.all_gather(w_back, 'dp', axis=1, tiled=True)  34.2 us
    all_gather x1, blocking collectives, on_device(): lax.all_gather(b_in, 'dp', axis=0, tiled=True)  23.2 us
  transfers between devices with their start and end apart: 11, of which 8 were waited for; matrix products, arithmetic and copies ran while one was open for 21% of the time, Pallas kernels for 0%

commit v1 on v0

--- a/solution.py
+++ b/solution.py
@@ -2,7 +2,10 @@
 
 import jax
 import jax.numpy as jnp
+import numpy as np
 from jax import lax
+from jax.experimental import pallas as pl
+from jax.experimental.pallas import tpu as pltpu
 from jax.sharding import PartitionSpec as P
 
 HD = 64
@@ -281,6 +284,816 @@
     )
 
 
+MESH = pl.DeviceIdType.MESH
+NZ = 4
+TILE = 256
+N_HEADS = TILE // HD
+NQ = 4
+NJ = 4
+NK = NQ + 2 * NJ
+VROWS = 56
+
+
+def fits_quad(mesh):
+    return mesh.shape["mp"] == 2 and mesh.shape["dp"] == 4 * NZ
+
+
+def dot_nn(a, b):
+    return lax.dot_general(a, b, (((1,), (0,)), ((), ())), preferred_element_type=jnp.float32)
+
+
+def dot_nt(a, b):
+    return lax.dot_general(a, b, (((1,), (1,)), ((), ())), preferred_element_type=jnp.float32)
+
+
+def dot_tn(a, b):
+    return lax.dot_general(a, b, (((0,), (0,)), ((), ())), preferred_element_type=jnp.float32)
+
+
+def layer_kernel(
+    bucket_ref,
+    counts_ref,
+    x_ref,
+    cot_ref,
+    gain_ref,
+    bias_ref,
+    bback_ref,
+    cos_ref,
+    sin_ref,
+    bin_ref,
+    wqkv_ref,
+    wot_ref,
+    win_ref,
+    wbt_ref,
+    block_ref,
+    gin_ref,
+    go_ref,
+    lng_ref,
+    lnb_ref,
+    bbk_ref,
+    gbin_ref,
+    B,
+    W,
+    NA,
+    SA,
+    NT,
+    ST,
+    CT,
+    SN,
+    BM,
+    QR,
+    KR,
+    VR,
+    DQ,
+    DK,
+    DV,
+    ATT,
+    DA,
+    ACT,
+    HG,
+    OUT,
+    DN,
+    GP,
+    GC,
+    RZ,
+    FS,
+    YS,
+    YR,
+    XH,
+    RSTD,
+    EXS,
+    EYS,
+    EXR,
+    EYR,
+    EXS2,
+    EYS2,
+    EXR2,
+    EYR2,
+    V,
+    VS,
+    VRV,
+    loc_sem,
+    ays,
+    ayr,
+    azs,
+    azr,
+    acs,
+    acr,
+    gs,
+    gr,
+    rcs,
+    rcr,
+    rzs,
+    rzr,
+    rys,
+    ryr,
+    exs,
+    exr,
+    vs,
+    vr,
+):
+    f32, bf16 = jnp.float32, jnp.bfloat16
+    dp, x = lax.axis_index("dp"), lax.axis_index("mp")
+    z = dp // 4
+    y = lax.rem(dp // 2, 2)
+    c = lax.rem(dp, 2)
+    rows = x_ref.shape[0]
+    width = x_ref.shape[1]
+    dev_x = (dp, 1 - x)
+    dev_y = (dp + 2 - 4 * y, x)
+    dev_c = (dp + 1 - 2 * c, x)
+    dev_r = (lax.rem(dp + 4, 4 * NZ), x)
+    dev_l = (lax.rem(dp + 4 * NZ - 4, 4 * NZ), x)
+    dev_z = [(lax.rem(dp + 4 * i, 4 * NZ), x) for i in (1, 2, 3)]
+    m_own = 2 * y + x
+    m_x = 2 * y + 1 - x
+    m_y = 2 - 2 * y + x
+    m_d = 3 - m_own
+
+    def rcp(src, dst, ss, rs, dev):
+        return pltpu.make_async_remote_copy(
+            src_ref=src, dst_ref=dst, send_sem=ss, recv_sem=rs, device_id=dev, device_id_type=MESH
+        )
+
+    barrier = pltpu.get_barrier_semaphore()
+    peers = [dev_x, dev_y, dev_c] + dev_z
+    for peer in peers:
+        pl.semaphore_signal(barrier, inc=1, device_id=peer, device_id_type=MESH)
+
+    def wsrc(k, q):
+        if k == NK:
+            return None
+        if k < 3:
+            return wqkv_ref.at[k, :, pl.ds(pl.multiple_of(q * TILE, TILE), TILE)]
+        if k == 3:
+            return wot_ref.at[:, pl.ds(pl.multiple_of(q * TILE, TILE), TILE)]
+        ref = win_ref if k % 2 == 0 else wbt_ref
+        j = (k - NQ) // 2
+        return ref.at[:, pl.ds(pl.multiple_of(q * (NJ * TILE) + j * TILE, TILE), TILE)]
+
+    def wv(k):
+        return B if isinstance(k, int) and k == NK else W.at[k]
+
+    def own_copy(k):
+        return pltpu.make_async_copy(wsrc(k, y), W.at[k, z, y, c], loc_sem.at[k])
+
+    def y_copy(k):
+        if k == NK:
+            return rcp(B.at[z, y, c], B.at[z, y, c], ays.at[k], ayr.at[k], dev_y)
+        return rcp(wsrc(k, 1 - y), W.at[k, z, y, c], ays.at[k], ayr.at[k], dev_y)
+
+    def y_arrived(k):
+        here = wv(k).at[z, 1 - y, c]
+        rcp(here, here, ays.at[k], ayr.at[k], dev_y).wait_recv()
+
+    def z_copy(k, way, s, e):
+        block = wv(k).at[e, :, c]
+        return rcp(
+            block, block, azs.at[k, way, s], azr.at[k, way, s], dev_r if way == 0 else dev_l
+        )
+
+    def c_copy(k, e):
+        block = wv(k).at[e, :, c]
+        return rcp(block, block, acs.at[k, e], acr.at[k, e], dev_c)
+
+    def ag_own(k, copied=True):
+        if copied:
+            pltpu.make_async_copy(
+                W.at[k, z, y, c], W.at[k, z, y, c], loc_sem.at[k]
+            ).wait()
+        y_arrived(k)
+
+        @pl.when(z < NZ - 1)
+        def _():
+            z_copy(k, 0, 0, z).start()
+
+        @pl.when(z > 0)
+        def _():
+            z_copy(k, 1, 0, z).start()
+
+        c_copy(k, z).start()
+
+    def ag_step(k, s):
+        @pl.when(z - 1 - s >= 0)
+        def _():
+            e = z - 1 - s
+            z_copy(k, 0, s, e).wait_recv()
+            if s < NZ - 2:
+
+                @pl.when(z < NZ - 1)
+                def _():
+                    z_copy(k, 0, s + 1, e).start()
+
+            c_copy(k, e).start()
+
+        @pl.when(z + 1 + s <= NZ - 1)
+        def _():
+            e = z + 1 + s
+            z_copy(k, 1, s, e).wait_recv()
+            if s < NZ - 2:
+
+                @pl.when(z > 0)
+                def _():
+                    z_copy(k, 1, s + 1, e).start()
+
+            c_copy(k, e).start()
+
+    def ag_done(k):
+        for e in range(NZ):
+            block = wv(k).at[e, :, 1 - c]
+            rcp(block, block, acs.at[k, e], acr.at[k, e], dev_c).wait_recv()
+
+    def ag_sent(k, copied=True):
+        y_copy(k).wait_send() if isinstance(k, int) else None
+        for s in range(NZ - 1):
+
+            @pl.when((z < NZ - 1) & (z - s >= 0))
+            def _():
+                z_copy(k, 0, s, z - s).wait_send()
+
+            @pl.when((z > 0) & (z + s <= NZ - 1))
+            def _():
+                z_copy(k, 1, s, z + s).wait_send()
+
+        for e in range(NZ):
+            c_copy(k, e).wait_send()
+
+    def ag_diag(t):
+        if t < NK:
+            ag_own(t)
+        for s in range(NZ - 1):
+            if 0 <= t - 1 - s < NK:
+                ag_step(t - 1 - s, s)
+
+    P0 = 64
+    parts = (pl.ds(0, P0), pl.ds(P0, rows - P0))
+    BUF = (NA, SA)
+
+    def g_copy(t, p, way, m):
+        block = BUF[t].at[m, parts[p]]
+        i = (t * 2 + p) * 3 + way
+        dev = (dev_x, dev_y)[way] if way < 2 else (dev_y, dev_x)[p]
+        return rcp(block, block, gs.at[i], gr.at[i], dev)
+
+    def g_send(t):
+        g_copy(t, 0, 0, m_own).start()
+        g_copy(t, 1, 1, m_own).start()
+        g_copy(t, 1, 0, m_own).start()
+        g_copy(t, 0, 1, m_own).start()
+
+    def g_forward(t):
+        g_copy(t, 0, 0, m_x).wait_recv()
+        g_copy(t, 0, 2, m_x).start()
+        g_copy(t, 1, 1, m_y).wait_recv()
+        g_copy(t, 1, 2, m_y).start()
+
+    def g_done(t):
+        g_copy(t, 1, 0, m_x).wait_recv()
+        g_copy(t, 0, 1, m_y).wait_recv()
+        g_copy(t, 0, 2, m_d).wait_recv()
+        g_copy(t, 1, 2, m_d).wait_recv()
+
+    def g_sent(t):
+        for p in (0, 1):
+            for way in (0, 1):
+                g_copy(t, p, way, m_own).wait_send()
+        g_copy(t, 0, 2, m_x).wait_send()
+        g_copy(t, 1, 2, m_y).wait_send()
+
+    def rs_c(k):
+        return rcp(GP.at[k, :, :, 1 - c], GC.at[k], rcs.at[k], rcr.at[k], dev_c)
+
+    def rs_z(k, way, e, slot):
+        return rcp(
+            GP.at[k, e, :, c],
+            RZ.at[k, slot],
+            rzs.at[k, e],
+            rzr.at[k, slot],
+            dev_r if way == 0 else dev_l,
+        )
+
+    def rs_begin(k):
+        rs_c(k).wait_recv()
+        for e in range(NZ):
+            GP[k, e, :, c] = (GP[k, e, :, c].astype(f32) + GC[k, e].astype(f32)).astype(bf16)
+
+        @pl.when(z == 0)
+        def _():
+            for e in range(NZ - 1, 0, -1):
+                rs_z(k, 0, e, e).start()
+
+        @pl.when(z == NZ - 1)
+        def _():
+            for e in range(NZ - 1):
+                rs_z(k, 1, e, e if e < NZ - 2 else 4).start()
+
+    def pass_on(k, way, e, slot):
+        rs_z(k, way, e, e).wait_recv()
+        GP[k, e, :, c] = (GP[k, e, :, c].astype(f32) + RZ[k, e].astype(f32)).astype(bf16)
+        rs_z(k, way, e, slot).start()
+
+    def rs_hop1(k):
+        @pl.when(z == 1)
+        def _():
+            pass_on(k, 0, 3, 3)
+            pass_on(k, 0, 2, 2)
+
+        @pl.when(z == 2)
+        def _():
+            pass_on(k, 1, 0, 0)
+            pass_on(k, 1, 1, 4)
+
+    def rs_hop2(k):
+        @pl.when(z == 2)
+        def _():
+            pass_on(k, 0, 3, 3)
+
+        @pl.when(z == 1)
+        def _():
+            pass_on(k, 1, 0, 4)
+
+    def rs_y(k):
+        return rcp(YS.at[k], YR.at[k], rys.at[k], ryr.at[k], dev_y)
+
+    def rs_final(k):
+        FS[...] = GP[k, z, :, c].astype(f32)
+
+        @pl.when(z > 0)
+        def _():
+            rs_z(k, 0, z, z).wait_recv()
+            FS[...] += RZ[k, z].astype(f32)
+
+        @pl.when(z < NZ - 1)
+        def _():
+            rs_z(k, 1, z, 4).wait_recv()
+            FS[...] += RZ[k, 4].astype(f32)
+
+        YS[k] = FS[1 - y].astype(bf16)
+        rs_y(k).start()
+        go_ref[k, y] = FS[y]
+
+    def rs_out(k):
+        rs_y(k).wait_recv()
+        go_ref[k, 1 - y] = YR[k].astype(f32)
+
+    def rs_sent(k):
+        rs_c(k).wait_send()
+        for e in range(NZ):
+
+            @pl.when(z != e)
+            def _():
+                rs_z(k, 0, e, e).wait_send()
+
+        rs_y(k).wait_send()
+
+    def e_copy(t, u, i):
+        src, dst, dev = (
+            (EXS, EXR, dev_x),
+            (EYS, EYR, dev_y),
+            (EXS2, EXR2, dev_x),
+            (EYS2, EYR2, dev_y),
+        )[i]
+        return rcp(src.at[t, u], dst.at[t, u], exs.at[t, u, i], exr.at[t, u, i], dev)
+
+    def cols(u, half):
+        return pl.ds(half * (width // 2) + u * TILE, TILE)
+
+    def e_first(t, u, P):
+        for i in range(2):
+            EXS[t, u, i] = P[2 * i + 1 - x, :, cols(u, 0)].astype(bf16)
+        e_copy(t, u, 0).start()
+        for i in range(2):
+            EYS[t, u, i] = P[2 - 2 * y + i, :, cols(u, 1)].astype(bf16)
+        e_copy(t, u, 1).start()
+
+    def e_second(t, u, P):
+        e_copy(t, u, 0).wait_recv()
+        EYS2[t, u] = (P[m_y, :, cols(u, 0)] + EXR[t, u, 1 - y].astype(f32)).astype(bf16)
+        e_copy(t, u, 3).start()
+        e_copy(t, u, 1).wait_recv()
+        EXS2[t, u] = (P[m_x, :, cols(u, 1)] + EYR[t, u, 1 - x].astype(f32)).astype(bf16)
+        e_copy(t, u, 2).start()
+
+    def e_last(t, u, P):
+        e_copy(t, u, 3).wait_recv()
+        P[m_own, :, cols(u, 0)] += EXR[t, u, y].astype(f32) + EYR2[t, u].astype(f32)
+        e_copy(t, u, 2).wait_recv()
+        P[m_own, :, cols(u, 1)] += EYR[t, u, x].astype(f32) + EXR2[t, u].astype(f32)
+
+    def e_sent(t):
+        for u in range(2):
+            for i in range(4):
+                e_copy(t, u, i).wait_send()
+
+    for k in range(NK):
+        own_copy(k).start()
+    xf = x_ref[...].astype(f32)
+    centred = xf - jnp.mean(xf, axis=-1, keepdims=True)
+    rstd = lax.rsqrt(jnp.mean(centred * centred, axis=-1, keepdims=True) + NORM_EPS)
+    xhat = centred * rstd
+    XH[...] = xhat
+    RSTD[...] = jnp.broadcast_to(rstd, RSTD.shape)
+    NA[m_own] = (xhat * gain_ref[...] + bias_ref[...]).astype(bf16)
+
+    bucket = bucket_ref[0]
+    B[z, y, c, 0:8] = jnp.broadcast_to(bin_ref[...].astype(f32), (8, 128)).astype(bf16)
+    B[z, y, c, 8:16] = jnp.full((8, 128), bucket.astype(f32), f32).astype(bf16)
+
+    pl.semaphore_wait(barrier, len(peers))
+    y_copy(NK).start()
+    for k in range(NQ):
+        y_copy(k).start()
+    g_send(0)
+
+    slot = lax.shift_right_logical(jnp.int32(rows), bucket)
+    shift_of = (rows.bit_length() - 1) - bucket
+    row = x * rows + lax.broadcasted_iota(jnp.int32, (rows, 128), 0)
+    slot_of = lax.shift_right_logical(row, jnp.full(row.shape, shift_of, jnp.int32))
+    place = row & jnp.full(row.shape, slot - 1, jnp.int32)
+    limit = jnp.zeros((rows, 128), jnp.int32)
+    for s in range(SLOTS):
+        limit = jnp.where(slot_of == s, counts_ref[s], limit)
+    valid = jnp.where(place < limit, 1.0, 0.0)[:, 0:1]
+    seeds = cot_ref[...].astype(f32) * valid
+    SA[m_own] = seeds.astype(bf16)
+    back_sum = jnp.sum(seeds, axis=0, keepdims=True)
+    V[...] = jnp.zeros_like(V)
+    for i in range(8):
+        V[16 + i : 17 + i, :] = back_sum[:, i * 128 : (i + 1) * 128]
+    for k in range(NQ, NK):
+        y_copy(k).start()
+    g_send(1)
+
+    ag_own(NK, copied=False)
+    for s in range(NZ - 1):
+        ag_step(NK, s)
+    g_forward(0)
+    for t in range(4):
+        ag_diag(t)
+    g_forward(1)
+    for t in range(4, NK + NZ - 1):
+        ag_diag(t)
+    ag_done(NK)
+    g_done(0)
+    g_done(1)
+    for k in range(NK):
+        ag_done(k)
+
+    lane = lax.broadcasted_iota(jnp.int32, (rows, TILE), 1)
+    even = (lane & 1) == 0
+    for g in range(2):
+        brow = B[z, g, c].astype(f32)[8:9, :]
+        ba = jnp.broadcast_to(brow, (rows, 128))
+
+        def pick(ref):
+            full = ref[...]
+            out = full
+            for b in range(1, 4):
+                n = rows >> b
+                out = jnp.where(ba == float(b), jnp.concatenate([full[:n]] * (1 << b), axis=0), out)
+            return out
+
+        cg, sg = pick(cos_ref), pick(sin_ref)
+        CT[g] = jnp.concatenate([cg, cg], axis=1)
+        SN[g] = jnp.concatenate([sg, sg], axis=1)
+        size = jnp.full((rows, 128), rows, jnp.int32)
+        for b in range(1, 4):
+            size = jnp.where(ba == float(b), rows >> b, size)
+        size = jnp.concatenate([size, size], axis=1)
+        qi = lax.broadcasted_iota(jnp.int32, (rows, rows), 0)
+        ki = lax.broadcasted_iota(jnp.int32, (rows, rows), 1)
+        BM[g] = jnp.where((ki <= qi) & ((qi ^ ki) < size), 0.0, MASKED_SCORE)
+
+    def turn(v, g, sign):
+        other = jnp.where(even, -pltpu.roll(v, TILE - 1, 1), pltpu.roll(v, 1, 1))
+        return v * CT[g] + (sign * other) * SN[g]
+
+    def flip(m, _):
+        cs = pl.ds(pl.multiple_of(m * rows, rows), rows)
+        for d in range(4):
+            NT[d, :, cs] = NA[m, :, d * TILE : (d + 1) * TILE].T
+            ST[d, :, cs] = SA[m, :, d * TILE : (d + 1) * TILE].T
+        return 0
+
+    lax.fori_loop(0, 4, flip, 0)
+
+    def weight(k):
+        return W[k].reshape(width, TILE)
+
+    scale = HD ** (-0.5)
+
+    def attend(m, _):
+        g = m // 2
+        nb = NA[m]
+        q = turn(dot_nn(nb, weight(0)), g, 1.0).astype(bf16)
+        kk = turn(dot_nn(nb, weight(1)), g, 1.0).astype(bf16)
+        v = dot_nn(nb, weight(2)).astype(bf16)
+        da = dot_nn(SA[m], weight(3)).astype(bf16)
+        QR[...] = q
+        KR[...] = kk
+        VR[...] = v
+        DA[...] = da
+        zero = jnp.zeros((rows, TILE), bf16)
+
+        def head(h, acc):
+            att, dq, dk, dv = acc
+            mine = (lane // HD) == h
+            qh = jnp.where(mine, QR[...], zero)
+            kh = jnp.where(mine, KR[...], zero)
+            vh = jnp.where(mine, VR[...], zero)
+            dh = jnp.where(mine, DA[...], zero)
+            s = dot_nt(qh, KR[...]) * scale + BM[g]
+            e = jnp.exp(s - jnp.max(s, axis=-1, keepdims=True))
+            p = e * (1.0 / jnp.sum(e, axis=-1, keepdims=True))
+            pb = p.astype(bf16)
+            att += dot_nn(pb, vh)
+            pg = dot_nt(dh, VR[...])
+            sg = p * (pg - jnp.sum(p * pg, axis=-1, keepdims=True))
+            sb = sg.astype(bf16)
+            dv += dot_tn(pb, dh)
+            dq += dot_nn(sb, kh)
+            dk += dot_tn(sb, qh)
+            return att, dq, dk, dv
+
+        none = jnp.zeros((rows, TILE), f32)
+        att, dq, dk, dv = lax.fori_loop(0, N_HEADS, head, (none,) * 4)
+        at = att.astype(bf16)
+        dqb = turn(dq * scale, g, -1.0).astype(bf16)
+        dkb = turn(dk * scale, g, -1.0).astype(bf16)
+        dvb = dv.astype(bf16)
+        rs = pl.ds(pl.multiple_of(m * rows, rows), rows)
+        ATT[rs, :] = at
+        DQ[rs, :] = dqb
+        DK[rs, :] = dkb
+        DV[rs, :] = dvb
+        OUT[m] = dot_nt(at, weight(3))
+        DN[m] = dot_nt(dqb, weight(0)) + dot_nt(dkb, weight(1)) + dot_nt(dvb, weight(2))
+        return 0
+
+    lax.fori_loop(0, 4, attend, 0)
+
+    def grad_of(k, left, right):
+        def block(d, _):
+            GP[k, d] = dot_nn(left[d], right[...]).astype(bf16).reshape(2, 2, 64, TILE)
+            return 0
+
+        lax.fori_loop(0, 4, block, 0)
+        rs_c(k).start()
+
+    grad_of(0, NT, DQ)
+    grad_of(1, NT, DK)
+    grad_of(2, NT, DV)
+    grad_of(3, ST, ATT)
+
+    def feed(j, _):
+        ki, kb = NQ + 2 * j, NQ + 1 + 2 * j
+        n0 = 2 * j
+        zz = 2 * y + n0 // 4
+        yy = lax.rem(n0 // 2, 2)
+        b0 = B[zz, yy, 0].astype(f32)[0:1, :]
+        b1 = B[zz, yy, 1].astype(f32)[0:1, :]
+        bias_j = jnp.concatenate([b0, b1], axis=1)
+
+        def rowsof(m, total):
+            u = dot_nn(NA[m], weight(ki)) + bias_j
+            u2 = u * u
+            k0 = float(np.sqrt(2.0 / np.pi))
+            t = jnp.tanh(k0 * u * (1.0 + 0.044715 * u2))
+            act = (0.5 * u * (1.0 + t)).astype(bf16)
+            slope = 0.5 * (1.0 + t) + (0.5 * k0) * u * (1.0 - t * t) * (1.0 + 0.134145 * u2)
+            hg = (dot_nn(SA[m], weight(kb)) * slope).astype(bf16)
+            rs = pl.ds(pl.multiple_of(m * rows, rows), rows)
+            ACT[rs, :] = act
+            HG[rs, :] = hg
+            OUT[m] += dot_nt(act, weight(kb))
+            DN[m] += dot_nt(hg, weight(ki))
+            return total + jnp.sum(hg.astype(f32), axis=0, keepdims=True)
+
+        total = lax.fori_loop(0, 4, rowsof, jnp.zeros((1, TILE), f32))
+        at = 24 + x * 16 + y * 8 + 2 * j
+        V[pl.ds(at, 1), :] = total[:, :128]
+        V[pl.ds(at + 1, 1), :] = total[:, 128:]
+        grad_of(ki, NT, HG)
+        grad_of(kb, ST, ACT)
+        return 0
+
+    lax.fori_loop(0, NJ, feed, 0)
+
+    for t, P in ((0, OUT), (1, DN)):
+        for u in range(2):
+            e_first(t, u, P)
+
+    def later(f):
+        lax.fori_loop(0, NK, lambda k, _: (f(k), 0)[1], 0)
+
+    later(rs_begin)
+    later(rs_hop1)
+    later(rs_hop2)
+    for t, P in ((0, OUT), (1, DN)):
+        for u in range(2):
+            e_second(t, u, P)
+        for u in range(2):
+            e_last(t, u, P)
+    block_ref[...] = (x_ref[...].astype(f32) + OUT[m_own] + bback_ref[...]).astype(bf16)
+    dn = DN[m_own]
+    xhat = XH[...]
+    e = dn * gain_ref[...]
+    me = jnp.mean(e, axis=-1, keepdims=True)
+    mex = jnp.mean(e * xhat, axis=-1, keepdims=True)
+    gin_ref[...] = (SA[m_own].astype(f32) + RSTD[:, 0:1] * (e - me - xhat * mex)).astype(bf16)
+    gsum = jnp.sum(dn * xhat, axis=0, keepdims=True)
+    bsum = jnp.sum(dn, axis=0, keepdims=True)
+    for i in range(8):
+        V[i : i + 1, :] = gsum[:, i * 128 : (i + 1) * 128]
+        V[8 + i : 9 + i, :] = bsum[:, i * 128 : (i + 1) * 128]
+
+    def v_copy(i, dev):
+        return rcp(VS.at[min(i, 3)], VRV.at[i], vs.at[i], vr.at[i], dev)
+
+    VS[0] = V[...]
+    for i, dev in enumerate((dev_c, dev_x, dev_y)):
+        v_copy(i, dev).start()
+        v_copy(i, dev).wait_recv()
+        VS[i + 1] = VS[i] + VRV[i]
+    for i, dev in enumerate(dev_z):
+        v_copy(3 + i, dev).start()
+    later(rs_final)
+    later(rs_out)
+    for i, dev in enumerate(dev_z):
+        v_copy(3 + i, dev).wait_recv()
+    V[...] = VS[3] + VRV[3] + VRV[4] + VRV[5]
+    index = 2 * dp + x
+    lane4 = lax.rem(index, 4)
+    for base, ref in ((0, lng_ref), (8, lnb_ref), (16, bbk_ref)):
+        line = V[pl.ds(base + index // 4, 1), :]
+        out = line[:, 0:32]
+        for n in range(1, 4):
+            out = jnp.where(lane4 == n, line[:, 32 * n : 32 * n + 32], out)
+        ref[...] = out
+    gbin_ref[...] = V[pl.ds(24 + 16 * x + dp, 1), :]
+
+    for k in range(NK + 1):
+        ag_sent(k)
+    for t in range(2):
+        g_sent(t)
+        e_sent(t)
+    later(rs_sent)
+    for i, dev in enumerate([dev_c, dev_x, dev_y] + dev_z):
+        v_copy(i, dev).wait_send()
+
+
+def rope_constants(rows):
+    half = np.arange(ROT // 2, dtype=np.float32)
+    rates = (10000.0 ** (-2.0 * half / ROT)).astype(np.float32)
+    angle = np.arange(rows, dtype=np.float32)[:, None] * rates[None, :]
+    angle = np.repeat(angle, 2, axis=1)
+    cos = np.concatenate([np.cos(angle), np.ones((rows, HD - ROT))], axis=1)
+    sin = np.concatenate([np.sin(angle), np.zeros((rows, HD - ROT))], axis=1)
+    two = lambda t: np.concatenate([t, t], axis=1).astype(np.float32)
+    return two(cos), two(sin)
+
+
+def on_quad(
+    residual_in,
+    cotangent,
+    ln_gain,
+    ln_bias,
+    w_qkv,
+    w_out,
+    w_in,
+    b_in,
+    w_back,
+    b_back,
+    bucket_ids,
+    residue_counts,
+):
+    rows, width = residual_in.shape
+    cos, sin = rope_constants(rows)
+    f32, bf16 = jnp.float32, jnp.bfloat16
+    vm = pl.BlockSpec(memory_space=pltpu.VMEM)
+    sm = pl.BlockSpec(memory_space=pltpu.SMEM)
+    anyspace = pl.BlockSpec(memory_space=pl.ANY)
+    shard = width // (4 * NZ)
+    sem = pltpu.SemaphoreType.DMA
+    block = (2, 2, rows, TILE)
+    outs = pl.pallas_call(
+        layer_kernel,
+        out_shape=(
+            jax.ShapeDtypeStruct((rows, width), bf16),
+            jax.ShapeDtypeStruct((rows, width), bf16),
+            jax.ShapeDtypeStruct((NK, 2, shard, TILE), f32),
+            jax.ShapeDtypeStruct((1, 32), f32),
+            jax.ShapeDtypeStruct((1, 32), f32),
+            jax.ShapeDtypeStruct((1, 32), f32),
+            jax.ShapeDtypeStruct((1, 128), f32),
+        ),
+        in_specs=[sm, sm] + [vm] * 8 + [anyspace] * 4,
+        out_specs=(vm,) * 7,
+        scratch_shapes=[
+            pltpu.VMEM((NZ, 2, 2, 16, 128), bf16),
+            pltpu.VMEM((NK, NZ, 2, 2, shard, TILE), bf16),
+            pltpu.VMEM((4, rows, width), bf16),
+            pltpu.VMEM((4, rows, width), bf16),
+            pltpu.VMEM((4, TILE, 4 * rows), bf16),
+            pltpu.VMEM((4, TILE, 4 * rows), bf16),
+            pltpu.VMEM((2, rows, TILE), f32),
+            pltpu.VMEM((2, rows, TILE), f32),
+            pltpu.VMEM((2, rows, rows), f32),
+            pltpu.VMEM((rows, TILE), bf16),
+            pltpu.VMEM((rows, TILE), bf16),
+            pltpu.VMEM((rows, TILE), bf16),
+            pltpu.VMEM((4 * rows, TILE), bf16),
+            pltpu.VMEM((4 * rows, TILE), bf16),
+            pltpu.VMEM((4 * rows, TILE), bf16),
+            pltpu.VMEM((4 * rows, TILE), bf16),
+            pltpu.VMEM((rows, TILE), bf16),
+            pltpu.VMEM((4 * rows, TILE), bf16),
+            pltpu.VMEM((4 * rows, TILE), bf16),
+            pltpu.VMEM((4, rows, width), f32),
+            pltpu.VMEM((4, rows, width), f32),
+            pltpu.VMEM((NK, NZ, 2, 2, shard, TILE), bf16),
+            pltpu.VMEM((NK, NZ, 2, shard, TILE), bf16),
+            pltpu.VMEM((NK, 5, 2, shard, TILE), bf16),
+            pltpu.VMEM((2, shard, TILE), f32),
+            pltpu.VMEM((NK, shard, TILE), bf16),
+            pltpu.VMEM((NK, shard, TILE), bf16),
+            pltpu.VMEM((rows, width), f32),
+            pltpu.VMEM((rows, 128), f32),
+            pltpu.VMEM((2,) + block, bf16),
+            pltpu.VMEM((2,) + block, bf16),
+            pltpu.VMEM((2,) + block, bf16),
+            pltpu.VMEM((2,) + block, bf16),
+            pltpu.VMEM((2, 2, rows, TILE), bf16),
+            pltpu.VMEM((2, 2, rows, TILE), bf16),
+            pltpu.VMEM((2, 2, rows, TILE), bf16),
+            pltpu.VMEM((2, 2, rows, TILE), bf16),
+            pltpu.VMEM((VROWS, 128), f32),
+            pltpu.VMEM((4, VROWS, 128), f32),
+            pltpu.VMEM((6, VROWS, 128), f32),
+            sem((NK,)),
+            sem((NK + 1,)),
+            sem((NK + 1,)),
+            sem((NK + 1, 2, 3)),
+            sem((NK + 1, 2, 3)),
+            sem((NK + 1, NZ)),
+            sem((NK + 1, NZ)),
+            sem((12,)),
+            sem((12,)),
+            sem((NK,)),
+            sem((NK,)),
+            sem((NK, NZ)),
+            sem((NK, 5)),
+            sem((NK,)),
+            sem((NK,)),
+            sem((2, 2, 4)),
+            sem((2, 2, 4)),
+            sem((6,)),
+            sem((6,)),
+        ],
+        compiler_params=pltpu.CompilerParams(
+            collective_id=0, has_side_effects=True, vmem_limit_bytes=63 << 20
+        ),
+        cost_estimate=pl.CostEstimate(
+            flops=20 * 2**30, bytes_accessed=8 * 2**20, transcendentals=2**21
+        ),
+    )(
+        bucket_ids,
+        residue_counts.reshape(SLOTS),
+        residual_in,
+        cotangent,
+        ln_gain.reshape(1, width),
+        ln_bias.reshape(1, width),
+        b_back.reshape(1, width),
+        jnp.asarray(cos),
+        jnp.asarray(sin),
+        b_in.reshape(1, 128),
+        w_qkv,
+        w_out.T,
+        w_in,
+        w_back.T,
+    )
+    block_out, grad_input, go, lng, lnb, bbk, gbin = outs
+    half = 2 * TILE
+    grad_w_qkv = go[:3].transpose(0, 2, 1, 3).reshape(3, shard, half)
+    grad_w_out = go[3].transpose(0, 2, 1).reshape(half, shard)
+    gi = go[NQ::2]
+    gb = go[NQ + 1 :: 2]
+    grad_w_in = gi.transpose(2, 1, 0, 3).reshape(shard, NJ * half)
+    grad_w_back = gb.transpose(1, 0, 3, 2).reshape(NJ * half, shard)
+    return (
+        block_out,
+        grad_input,
+        lng.reshape(32),
+        lnb.reshape(32),
+        grad_w_qkv,
+        grad_w_out,
+        grad_w_in,
+        gbin.reshape(128),
+        grad_w_back,
+        bbk.reshape(32),
+    )
+
+
 def solution(mesh):
     placed = (
         P(("dp", "mp"), None),
@@ -297,7 +1110,7 @@
         P("dp", None),
     )
     return jax.shard_map(
-        on_device,
+        on_quad if fits_quad(mesh) else on_device,
         mesh=mesh,
         in_specs=placed,
         out_specs=(

time: 603 us -> 235 us (0.39)
  the two profiles are of different devices: /device:TPU:0 before, /device:TPU:8 now
where the time goes in v1:
time: 235 us; the launch traced here: 234 us
  Pallas kernels  222 us (94%)
  local copies, waits for them, and re-layouts  11.2 us (5%)
    pallas_call x1, Pallas kernels, on_quad(): pl.pallas_call(layer_kernel, out_shape=(jax.ShapeDtypeStruct((rows, width...  222 us
    unnamed x20, local copies, waits for them, and re-layouts  5.59 us

profile of v1, /device:TPU:8, one launch (start us, length us, event | category | flops | bytes accessed | tf_op | source)
XLA Modules:
  0.0 234.3 jit_solution(5541459106263258027)
XLA Ops:
  1.3 221.8 %shard_map.213 = (bf16[256,1024]{1,0:T(8,128)(2,1)}, bf16[256,1024]{1,0:T(8,128)(2,1)}, f32[12,2,64,256]{3,2,1,0:T(8,128)}, f32[1,32]{1,0:T(1,128)}, f32[1,32]{1...) custom-call(s32[1]{0:T(128)S(6)} %copy.36.bucket_ref, s32[16]{0:T(128)} %bitcast.34, bf16[256,1024]{1,0:T(8,128)(2,1)} %x_ref.1, ...), custom_call_target="tpu_custom_call" | custom-call | flops 21474836480 | bytes 8388608 | tf_op jit(solution)/shard_map/pallas_call | solution.py:979
  223.1 0.9 slice_bitcast_fusion.3
  224.0 0.7 copy.29
  224.6 1.0 slice_bitcast_fusion.2
  225.7 1.3 slice_bitcast_fusion
  227.0 0.3 copy.27
  227.3 1.1 reshape.70
  228.4 0.0 copy-start.1
  228.4 0.8 copy.28
  229.2 0.0 copy-start
  229.2 0.3 copy.26
  229.5 0.0 copy-start.5
  229.5 0.0 copy-start.4
  229.5 0.0 copy-start.3
  229.6 0.0 copy-start.2
  229.6 1.1 reshape.68
  230.6 0.0 copy-done.1
  230.6 0.8 copy.37
  231.4 0.0 copy-done
  231.4 0.8 copy.38
  232.2 0.0 copy-done.5
  232.2 0.5 copy.39
  232.7 0.0 copy-done.4
  232.7 0.5 copy.40
  233.3 0.0 copy-done.3
  233.3 0.5 copy.41
  233.8 0.0 copy-done.2
  233.8 0.5 copy.42
Async XLA Ops:
  228.4 2.2 copy-start.1
  229.2 2.2 copy-start
  229.5 2.7 %copy-start.5 = (f32[1,32]{1,0:T(1,128)S(1)}, f32[1,32]{1,0:T(1,128)}, u32[]{:S(2)}) copy-start(f32[1,32]{1,0:T(1,128)} %get-tuple-element.19) | copy-start | bytes 388
  229.5 3.2 %copy-start.4 = (f32[1,32]{1,0:T(1,128)S(1)}, f32[1,32]{1,0:T(1,128)}, u32[]{:S(2)}) copy-start(f32[1,32]{1,0:T(1,128)} %get-tuple-element.20) | copy-start | bytes 388
  229.5 3.7 %copy-start.3 = (f32[1,128]{1,0:T(1,128)S(1)}, f32[1,128]{1,0:T(1,128)}, u32[]{:S(2)}) copy-start(f32[1,128]{1,0:T(1,128)} %get-tuple-element.22) | copy-start | bytes 1540
  229.6 4.2 %copy-start.2 = (f32[1,32]{1,0:T(1,128)S(1)}, f32[1,32]{1,0:T(1,128)}, u32[]{:S(2)}) copy-start(f32[1,32]{1,0:T(1,128)} %get-tuple-element.23) | copy-start | bytes 388

commit v2 on v1

--- a/solution.py
+++ b/solution.py
@@ -423,12 +423,12 @@
     def wsrc(k, q):
         if k == NK:
             return None
-        if k < 3:
-            return wqkv_ref.at[k, :, pl.ds(pl.multiple_of(q * TILE, TILE), TILE)]
-        if k == 3:
+        if 2 <= k < 5:
+            return wqkv_ref.at[k - 2, :, pl.ds(pl.multiple_of(q * TILE, TILE), TILE)]
+        if k == 5:
             return wot_ref.at[:, pl.ds(pl.multiple_of(q * TILE, TILE), TILE)]
         ref = win_ref if k % 2 == 0 else wbt_ref
-        j = (k - NQ) // 2
+        j = 0 if k < 2 else (k - NQ) // 2
         return ref.at[:, pl.ds(pl.multiple_of(q * (NJ * TILE) + j * TILE, TILE), TILE)]
 
     def wv(k):
@@ -518,12 +518,20 @@
         for e in range(NZ):
             c_copy(k, e).wait_send()
 
-    def ag_diag(t):
-        if t < NK:
-            ag_own(t)
+    order = [NK] + list(range(NK))
+    turns = iter(range(NK + NZ))
+
+    def ag_turn():
+        t = next(turns, None)
+        if t is None:
+            return
+        if t + 3 <= NK:
+            y_copy(order[t + 3]).start()
+        if t <= NK:
+            ag_own(order[t], copied=t > 0)
         for s in range(NZ - 1):
-            if 0 <= t - 1 - s < NK:
-                ag_step(t - 1 - s, s)
+            if 0 <= t - 1 - s <= NK:
+                ag_step(order[t - 1 - s], s)
 
     P0 = 64
     parts = (pl.ds(0, P0), pl.ds(P0, rows - P0))
@@ -541,15 +549,19 @@
         g_copy(t, 1, 0, m_own).start()
         g_copy(t, 0, 1, m_own).start()
 
+    def g_near(t):
+        g_copy(t, 0, 0, m_x).wait_recv()
+        g_copy(t, 1, 1, m_y).wait_recv()
+
     def g_forward(t):
-        g_copy(t, 0, 0, m_x).wait_recv()
         g_copy(t, 0, 2, m_x).start()
-        g_copy(t, 1, 1, m_y).wait_recv()
         g_copy(t, 1, 2, m_y).start()
 
-    def g_done(t):
+    def g_rest(t):
         g_copy(t, 1, 0, m_x).wait_recv()
         g_copy(t, 0, 1, m_y).wait_recv()
+
+    def g_far(t):
         g_copy(t, 0, 2, m_d).wait_recv()
         g_copy(t, 1, 2, m_d).wait_recv()
 
@@ -635,6 +647,16 @@
     def rs_out(k):
         rs_y(k).wait_recv()
         go_ref[k, 1 - y] = YR[k].astype(f32)
+
+    rturns = iter(range(NK + 4))
+
+    def rs_turn():
+        r = next(rturns, None)
+        if r is None:
+            return
+        for s, f in enumerate((rs_begin, rs_hop1, rs_hop2, rs_final, rs_out)):
+            if 0 <= r - s < NK:
+                f(r - s)
 
     def rs_sent(k):
         rs_c(k).wait_send()
@@ -700,8 +722,7 @@
     B[z, y, c, 8:16] = jnp.full((8, 128), bucket.astype(f32), f32).astype(bf16)
 
     pl.semaphore_wait(barrier, len(peers))
-    y_copy(NK).start()
-    for k in range(NQ):
+    for k in order[:3]:
         y_copy(k).start()
     g_send(0)
 
@@ -720,24 +741,8 @@
     V[...] = jnp.zeros_like(V)
     for i in range(8):
         V[16 + i : 17 + i, :] = back_sum[:, i * 128 : (i + 1) * 128]
-    for k in range(NQ, NK):
-        y_copy(k).start()
-    g_send(1)
-
-    ag_own(NK, copied=False)
-    for s in range(NZ - 1):
-        ag_step(NK, s)
-    g_forward(0)
-    for t in range(4):
-        ag_diag(t)
-    g_forward(1)
-    for t in range(4, NK + NZ - 1):
-        ag_diag(t)
-    ag_done(NK)
-    g_done(0)
-    g_done(1)
-    for k in range(NK):
-        ag_done(k)
+    ag_turn()
+    ag_turn()
 
     lane = lax.broadcasted_iota(jnp.int32, (rows, TILE), 1)
     even = (lane & 1) == 0
@@ -768,27 +773,23 @@
         other = jnp.where(even, -pltpu.roll(v, TILE - 1, 1), pltpu.roll(v, 1, 1))
         return v * CT[g] + (sign * other) * SN[g]
 
-    def flip(m, _):
+    def flip(src, dst, m):
         cs = pl.ds(pl.multiple_of(m * rows, rows), rows)
         for d in range(4):
-            NT[d, :, cs] = NA[m, :, d * TILE : (d + 1) * TILE].T
-            ST[d, :, cs] = SA[m, :, d * TILE : (d + 1) * TILE].T
-        return 0
-
-    lax.fori_loop(0, 4, flip, 0)
+            dst[d, :, cs] = src[m, :, d * TILE : (d + 1) * TILE].T
 
     def weight(k):
         return W[k].reshape(width, TILE)
 
     scale = HD ** (-0.5)
 
-    def attend(m, _):
+    def attend(m):
         g = m // 2
         nb = NA[m]
-        q = turn(dot_nn(nb, weight(0)), g, 1.0).astype(bf16)
-        kk = turn(dot_nn(nb, weight(1)), g, 1.0).astype(bf16)
-        v = dot_nn(nb, weight(2)).astype(bf16)
-        da = dot_nn(SA[m], weight(3)).astype(bf16)
+        q = turn(dot_nn(nb, weight(2)), g, 1.0).astype(bf16)
+        kk = turn(dot_nn(nb, weight(3)), g, 1.0).astype(bf16)
+        v = dot_nn(nb, weight(4)).astype(bf16)
+        da = dot_nn(SA[m], weight(5)).astype(bf16)
         QR[...] = q
         KR[...] = kk
         VR[...] = v
@@ -816,7 +817,9 @@
             return att, dq, dk, dv
 
         none = jnp.zeros((rows, TILE), f32)
-        att, dq, dk, dv = lax.fori_loop(0, N_HEADS, head, (none,) * 4)
+        acc = lax.fori_loop(0, N_HEADS // 2, head, (none,) * 4)
+        ag_turn()
+        att, dq, dk, dv = lax.fori_loop(N_HEADS // 2, N_HEADS, head, acc)
         at = att.astype(bf16)
         dqb = turn(dq * scale, g, -1.0).astype(bf16)
         dkb = turn(dk * scale, g, -1.0).astype(bf16)
@@ -826,11 +829,8 @@
         DQ[rs, :] = dqb
         DK[rs, :] = dkb
         DV[rs, :] = dvb
-        OUT[m] = dot_nt(at, weight(3))
-        DN[m] = dot_nt(dqb, weight(0)) + dot_nt(dkb, weight(1)) + dot_nt(dvb, weight(2))
-        return 0
-
-    lax.fori_loop(0, 4, attend, 0)
+        OUT[m] += dot_nt(at, weight(5))
+        DN[m] += dot_nt(dqb, weight(2)) + dot_nt(dkb, weight(3)) + dot_nt(dvb, weight(4))
 
     def grad_of(k, left, right):
         def block(d, _):
@@ -840,44 +840,110 @@
         lax.fori_loop(0, 4, block, 0)
         rs_c(k).start()
 
-    grad_of(0, NT, DQ)
-    grad_of(1, NT, DK)
-    grad_of(2, NT, DV)
-    grad_of(3, ST, ATT)
-
-    def feed(j, _):
-        ki, kb = NQ + 2 * j, NQ + 1 + 2 * j
-        n0 = 2 * j
-        zz = 2 * y + n0 // 4
-        yy = lax.rem(n0 // 2, 2)
-        b0 = B[zz, yy, 0].astype(f32)[0:1, :]
-        b1 = B[zz, yy, 1].astype(f32)[0:1, :]
-        bias_j = jnp.concatenate([b0, b1], axis=1)
-
-        def rowsof(m, total):
-            u = dot_nn(NA[m], weight(ki)) + bias_j
-            u2 = u * u
-            k0 = float(np.sqrt(2.0 / np.pi))
-            t = jnp.tanh(k0 * u * (1.0 + 0.044715 * u2))
-            act = (0.5 * u * (1.0 + t)).astype(bf16)
-            slope = 0.5 * (1.0 + t) + (0.5 * k0) * u * (1.0 - t * t) * (1.0 + 0.134145 * u2)
-            hg = (dot_nn(SA[m], weight(kb)) * slope).astype(bf16)
-            rs = pl.ds(pl.multiple_of(m * rows, rows), rows)
-            ACT[rs, :] = act
-            HG[rs, :] = hg
-            OUT[m] += dot_nt(act, weight(kb))
-            DN[m] += dot_nt(hg, weight(ki))
-            return total + jnp.sum(hg.astype(f32), axis=0, keepdims=True)
-
-        total = lax.fori_loop(0, 4, rowsof, jnp.zeros((1, TILE), f32))
+    def slice_of(j):
+        return (0, 1) if j == 0 else (NQ + 2 * j, NQ + 1 + 2 * j)
+
+    def feed(j, m, first=False):
+        ki, kb = slice_of(j)
+        b0 = B[2 * y + j // 2, j % 2, 0].astype(f32)[0:1, :]
+        b1 = B[2 * y + j // 2, j % 2, 1].astype(f32)[0:1, :]
+        u = dot_nn(NA[m], weight(ki)) + jnp.concatenate([b0, b1], axis=1)
+        u2 = u * u
+        k0 = float(np.sqrt(2.0 / np.pi))
+        t = jnp.tanh(k0 * u * (1.0 + 0.044715 * u2))
+        act = (0.5 * u * (1.0 + t)).astype(bf16)
+        slope = 0.5 * (1.0 + t) + (0.5 * k0) * u * (1.0 - t * t) * (1.0 + 0.134145 * u2)
+        hg = (dot_nn(SA[m], weight(kb)) * slope).astype(bf16)
+        rs = pl.ds(pl.multiple_of(m * rows, rows), rows)
+        ACT[rs, :] = act
+        HG[rs, :] = hg
+        out, dn = dot_nt(act, weight(kb)), dot_nt(hg, weight(ki))
+        if first:
+            OUT[m] = out
+            DN[m] = dn
+        else:
+            OUT[m] += out
+            DN[m] += dn
         at = 24 + x * 16 + y * 8 + 2 * j
-        V[pl.ds(at, 1), :] = total[:, :128]
-        V[pl.ds(at + 1, 1), :] = total[:, 128:]
+        total = jnp.sum(hg.astype(f32), axis=0, keepdims=True)
+        V[pl.ds(at, 1), :] += total[:, :128]
+        V[pl.ds(at + 1, 1), :] += total[:, 128:]
+
+    def feed_grads(j):
+        ki, kb = slice_of(j)
         grad_of(ki, NT, HG)
         grad_of(kb, ST, ACT)
-        return 0
-
-    lax.fori_loop(0, NJ, feed, 0)
+
+    def feed_rows(j):
+        for i in (0, 1):
+            lax.fori_loop(2 * i, 2 * i + 2, lambda m, _: (feed(j, m), 0)[1], 0)
+            ag_turn()
+
+    def arrived(*chunks):
+        for k in chunks:
+            ag_done(k)
+
+    flip(NA, NT, m_own)
+    flip(SA, ST, m_own)
+    ag_turn()
+    g_near(0)
+    g_send(1)
+    g_forward(0)
+    ag_turn()
+    ag_turn()
+    ag_turn()
+    arrived(NK, 0, 1)
+    feed(0, m_own, True)
+    g_rest(0)
+    flip(NA, NT, m_x)
+    flip(NA, NT, m_y)
+    ag_turn()
+    g_near(1)
+    g_forward(1)
+    g_rest(1)
+    feed(0, m_x, True)
+    feed(0, m_y, True)
+    flip(SA, ST, m_x)
+    flip(SA, ST, m_y)
+    ag_turn()
+    ag_turn()
+    ag_turn()
+    arrived(2, 3, 4, 5)
+    attend(m_own)
+    ag_turn()
+    attend(m_x)
+    g_far(0)
+    flip(NA, NT, m_d)
+    attend(m_y)
+    g_far(1)
+    flip(SA, ST, m_d)
+    feed(0, m_d, True)
+    feed_grads(0)
+    attend(m_d)
+    ag_turn()
+    rs_turn()
+    grad_of(2, NT, DQ)
+    grad_of(3, NT, DK)
+    rs_turn()
+    grad_of(4, NT, DV)
+    grad_of(5, ST, ATT)
+    ag_turn()
+    rs_turn()
+    arrived(6, 7)
+    feed_rows(1)
+    rs_turn()
+    feed_grads(1)
+    rs_turn()
+    arrived(8, 9)
+    feed_rows(2)
+    rs_turn()
+    feed_grads(2)
+    rs_turn()
+    ag_turn()
+    ag_turn()
+    arrived(10, 11)
+    feed_rows(3)
+    rs_turn()
 
     for t, P in ((0, OUT), (1, DN)):
         for u in range(2):
@@ -886,12 +952,19 @@
     def later(f):
         lax.fori_loop(0, NK, lambda k, _: (f(k), 0)[1], 0)
 
-    later(rs_begin)
-    later(rs_hop1)
-    later(rs_hop2)
+    feed_grads(3)
+    rs_turn()
+    e_second(0, 0, OUT)
+    rs_turn()
+    e_second(0, 1, OUT)
+    rs_turn()
+    rs_turn()
+    e_second(1, 0, DN)
+    rs_turn()
+    e_second(1, 1, DN)
+    for _ in range(NK + 4):
+        rs_turn()
     for t, P in ((0, OUT), (1, DN)):
-        for u in range(2):
-            e_second(t, u, P)
         for u in range(2):
             e_last(t, u, P)
     block_ref[...] = (x_ref[...].astype(f32) + OUT[m_own] + bback_ref[...]).astype(bf16)
@@ -917,8 +990,6 @@
         VS[i + 1] = VS[i] + VRV[i]
     for i, dev in enumerate(dev_z):
         v_copy(3 + i, dev).start()
-    later(rs_final)
-    later(rs_out)
     for i, dev in enumerate(dev_z):
         v_copy(3 + i, dev).wait_recv()
     V[...] = VS[3] + VRV[3] + VRV[4] + VRV[5]
@@ -1074,10 +1145,10 @@
     )
     block_out, grad_input, go, lng, lnb, bbk, gbin = outs
     half = 2 * TILE
-    grad_w_qkv = go[:3].transpose(0, 2, 1, 3).reshape(3, shard, half)
-    grad_w_out = go[3].transpose(0, 2, 1).reshape(half, shard)
-    gi = go[NQ::2]
-    gb = go[NQ + 1 :: 2]
+    grad_w_qkv = go[2:5].transpose(0, 2, 1, 3).reshape(3, shard, half)
+    grad_w_out = go[5].transpose(0, 2, 1).reshape(half, shard)
+    gi = jnp.concatenate([go[0:1], go[6::2]])
+    gb = jnp.concatenate([go[1:2], go[7::2]])
     grad_w_in = gi.transpose(2, 1, 0, 3).reshape(shard, NJ * half)
     grad_w_back = gb.transpose(1, 0, 3, 2).reshape(NJ * half, shard)
     return (

time: 235 us -> 184 us (0.78)
  the two profiles are of different devices: /device:TPU:8 before, /device:TPU:0 now
where the time goes in v2:
time: 184 us
  Pallas kernels  172 us (93%)
  local copies, waits for them, and re-layouts  10.3 us (6%)
    pallas_call x1, Pallas kernels, on_quad(): pl.pallas_call(layer_kernel, out_shape=(jax.ShapeDtypeStruct((rows, width...  172 us

profile of v2, /device:TPU:0, one launch (start us, length us, event | category | flops | bytes accessed | tf_op | source)
XLA Modules:
  0.0 184.2 jit_solution(7035474392933251210)
XLA Ops:
  1.3 172.4 %shard_map.213 = (bf16[256,1024]{1,0:T(8,128)(2,1)}, bf16[256,1024]{1,0:T(8,128)(2,1)}, f32[12,2,64,256]{3,2,1,0:T(8,128)}, f32[1,32]{1,0:T(1,128)}, f32[1,32]{1...) custom-call(s32[1]{0:T(128)S(6)} %copy.36.bucket_ref, s32[16]{0:T(128)} %bitcast.34, bf16[256,1024]{1,0:T(8,128)(2,1)} %x_ref.1, ...), custom_call_target="tpu_custom_call" | custom-call | flops 21474836480 | bytes 8388608 | tf_op jit(solution)/shard_map/pallas_call | solution.py:1050
  173.7 1.1 fusion
  174.8 1.3 fusion.1
  176.2 0.1 maximum_bitcast_fusion
  176.3 0.3 copy.26
  176.6 1.1 reshape.68
  177.7 0.0 copy-start.1
  177.7 0.7 copy.29
  178.3 0.8 copy.28
  179.1 0.0 copy-start
  179.1 0.3 copy.27
  179.5 0.0 copy-start.5
  179.5 0.0 copy-start.4
  179.5 0.0 copy-start.3
  179.5 0.0 copy-start.2
  179.5 1.1 reshape.70
  180.6 0.0 copy-done.1
  180.6 0.8 copy.37
  181.4 0.0 copy-done
  181.4 0.8 copy.38
  182.2 0.0 copy-done.5
  182.2 0.5 copy.39
  182.7 0.0 copy-done.4
  182.7 0.5 copy.40
  183.2 0.0 copy-done.3
  183.2 0.5 copy.41
  183.7 0.0 copy-done.2
  183.7 0.5 copy.42
Async XLA Ops:
  177.7 2.9 %copy-start.1 = (bf16[256,1024]{1,0:T(8,128)(2,1)S(1)}, bf16[256,1024]{1,0:T(8,128)(2,1)}, u32[]{:S(2)}) copy-start(bf16[256,1024]{1,0:T(8,128)(2,1)} %get-tuple-element.42) | copy-start | bytes 1572868
  179.1 2.2 %copy-start = (bf16[256,1024]{1,0:T(8,128)(2,1)S(1)}, bf16[256,1024]{1,0:T(8,128)(2,1)}, u32[]{:S(2)}) copy-start(bf16[256,1024]{1,0:T(8,128)(2,1)} %get-tuple-element.43) | copy-start | bytes 1572868
  179.5 2.7 %copy-start.5 = (f32[1,32]{1,0:T(1,128)S(1)}, f32[1,32]{1,0:T(1,128)}, u32[]{:S(2)}) copy-start(f32[1,32]{1,0:T(1,128)} %get-tuple-element.19) | copy-start | bytes 388
  179.5 3.2 %copy-start.4 = (f32[1,32]{1,0:T(1,128)S(1)}, f32[1,32]{1,0:T(1,128)}, u32[]{:S(2)}) copy-start(f32[1,32]{1,0:T(1,128)} %get-tuple-element.20) | copy-start | bytes 388
  179.5 3.7 %copy-start.3 = (f32[1,128]{1,0:T(1,128)S(1)}, f32[1,128]{1,0:T(1,128)}, u32[]{:S(2)}) copy-start(f32[1,128]{1,0:T(1,128)} %get-tuple-element.22) | copy-start | bytes 1540
  179.5 4.2 %copy-start.2 = (f32[1,32]{1,0:T(1,128)S(1)}, f32[1,32]{1,0:T(1,128)}, u32[]{:S(2)}) copy-start(f32[1,32]{1,0:T(1,128)} %get-tuple-element.23) | copy-start | bytes 388
